TPU v7x, 32 devices: a whole 2x2x4 slice. The times are simulated.
32 devices in a mesh: groups: 2 (over y), dp: 4 (over z), tensor: 4 (over x, core).
Axes of the slice: x: 2, y: 2, z: 4, core: 2. Of those that a mesh axis runs over, the one named last changes fastest.
Arguments:
- x_inner: bfloat16 [2048, 8192], P(('groups', 'dp'), 'tensor'), parts along dimension 0, may hold values from -6 to 6
- log_decay: float32 [2048, 128], P(('groups', 'dp'), 'tensor'), parts along dimension 0, may hold values from -2.5 to 0, as said below
- in_map: float32 [2048, 16], P(('groups', 'dp')), parts along dimension 0, may hold values from -6 to 6
- out_map: float32 [2048, 16], P(('groups', 'dp')), parts along dimension 0, may hold values from -0.125 to 0.125
- grad_out: bfloat16 [2048, 8192], P(('groups', 'dp'), 'tensor'), parts along dimension 0, may hold values from -6 to 6
Outputs:
- scan_out: bfloat16 [2048, 8192], P(('groups', 'dp'), 'tensor'), parts along dimension 0
- grad_inner: bfloat16 [2048, 8192], P(('groups', 'dp'), 'tensor'), parts along dimension 0
- grad_decay: float32 [2048, 128], P(('groups', 'dp'), 'tensor'), parts along dimension 0
- grad_in_map: float32 [2048, 16], P(('groups', 'dp')), parts along dimension 0
- output_map_gradient: float32 [2048, 16], P(('groups', 'dp')), parts along dimension 0
There are 2 independent parts, one for each index of `groups`. A program takes and returns all parts, laid end to end along the dimension named above; each array names one. Nothing has to cross between parts.
Inputs may be any that keep to these rules, and one draw needn't show every extreme that they name: log_decay is negative.
All inputs are finite; a program needn't handle non-finite values.
Results may differ from a plain program's by a relative error of at most 0.012.
Values sent between devices are 32-bit elements; how exact they have to be, the bound alone decides.
A program may use at most 128 MiB of HBM per device.

v0:
```python
import jax
import jax.numpy as jnp
from jax import lax
from jax.sharding import PartitionSpec as P

BLOCK = 128


def carried_in(part, axis, combine, identity, reverse):
    count = lax.axis_size(axis)
    place = lax.axis_index(axis)
    ahead = count - 1 - place if reverse else place
    gathered = jax.tree.map(lambda a: lax.all_gather(a, axis), part)
    state = jax.tree.map(lambda a, e: jnp.zeros_like(a) + jnp.asarray(e, a.dtype), part, identity)

    def one(hop, state):
        source = count - 1 - hop if reverse else hop
        return combine(
            state, jax.tree.map(lambda a: lax.dynamic_index_in_dim(a, source, 0, False), gathered)
        )

    return lax.fori_loop(0, ahead, one, state)


def block_pass(carry_state, pieces):
    inputs, decays, in_rows, out_rows = pieces
    cumulative = jnp.cumsum(decays, axis=0)
    length = decays.shape[0]
    causal = jnp.arange(length)[:, None] >= jnp.arange(length)[None, :]
    by_head = cumulative.T
    spread = by_head[:, :, None] - by_head[:, None, :]
    weights = jnp.exp(jnp.where(causal[None, :, :], spread, -1e30))
    scores = jnp.dot(
        out_rows, in_rows.T, preferred_element_type=jnp.float32, precision=lax.Precision.HIGHEST
    )
    mixing = weights * scores[None, :, :]
    within = jnp.einsum("hts,shp->thp", mixing, inputs, preferred_element_type=jnp.float32)
    carried = jnp.exp(cumulative)[:, :, None] * jnp.einsum(
        "tn,hpn->thp", out_rows, carry_state, preferred_element_type=jnp.float32
    )
    tail_decay = jnp.exp(cumulative[-1][None, :] - cumulative)
    new_state = jnp.exp(cumulative[-1])[:, None, None] * carry_state + jnp.einsum(
        "sh,shp,sn->hpn", tail_decay, inputs, in_rows, preferred_element_type=jnp.float32
    )
    return (new_state, within + carried)


def run_rows(inputs, decays, in_rows, out_rows, carry_state, block_len):
    row_count = inputs.shape[0]
    head_count = decays.shape[1]
    head_width = carry_state.shape[1]
    count_of_blocks = row_count // block_len
    pieces = (
        inputs.reshape(count_of_blocks, block_len, head_count, head_width),
        decays.reshape(count_of_blocks, block_len, head_count),
        in_rows.reshape(count_of_blocks, block_len, -1),
        out_rows.reshape(count_of_blocks, block_len, -1),
    )
    last_state, outputs = lax.scan(jax.checkpoint(block_pass), carry_state, pieces)
    return (outputs.reshape(row_count, head_count * head_width), last_state)


def merge_segment_pairs(earlier_pair, later_pair):
    return (
        earlier_pair[0] * later_pair[0],
        later_pair[0][:, None, None] * earlier_pair[1] + later_pair[1],
    )


def carry_back(through, local_term):
    identity = (jnp.ones_like(through), jnp.zeros_like(local_term))
    result = carried_in((through, local_term), "dp", merge_segment_pairs, identity, True)
    return result[1]


def local(x_inner, log_decay, in_map, out_map, grad_out):
    row_count = x_inner.shape[0]
    head_count = log_decay.shape[1]
    head_width = x_inner.shape[1] // head_count
    inputs = x_inner.astype(jnp.float32)
    cotangent = grad_out.astype(jnp.float32)
    cumulative = jnp.cumsum(log_decay, axis=0)
    total_decay = cumulative[-1]
    own_state = jnp.einsum(
        "sh,shp,sn->hpn",
        jnp.exp(total_decay[None, :] - cumulative),
        inputs.reshape(row_count, head_count, head_width),
        in_map,
        preferred_element_type=jnp.float32,
    )
    through = jnp.exp(total_decay)
    identity = (jnp.ones_like(through), jnp.zeros_like(own_state))
    prefix = carried_in((through, own_state), "dp", merge_segment_pairs, identity, False)
    state_in = prefix[1]

    def forward(inputs_arg, decays_arg, in_arg, out_arg, start_state):
        return run_rows(inputs_arg, decays_arg, in_arg, out_arg, start_state, BLOCK)

    (outputs, last_state), pullback = jax.vjp(forward, inputs, log_decay, in_map, out_map, state_in)
    first_grads = pullback((cotangent, jnp.zeros_like(last_state)))
    state_out = carry_back(through, first_grads[4])
    second_grads = pullback((jnp.zeros_like(cotangent), state_out))
    gradients = jax.tree.map(jnp.add, first_grads, second_grads)
    shared_in, shared_out = lax.psum((gradients[2], gradients[3]), "tensor")
    return (
        outputs.astype(jnp.bfloat16),
        gradients[0].astype(jnp.bfloat16),
        gradients[1],
        shared_in,
        shared_out,
    )


def solution(mesh):
    placed = (
        P(("groups", "dp"), "tensor"),
        P(("groups", "dp"), "tensor"),
        P(("groups", "dp"), None),
        P(("groups", "dp"), None),
        P(("groups", "dp"), "tensor"),
    )
    return jax.shard_map(
        local,
        mesh=mesh,
        in_specs=placed,
        out_specs=(
            P(("groups", "dp"), "tensor"),
            P(("groups", "dp"), "tensor"),
            P(("groups", "dp"), "tensor"),
            P(("groups", "dp"), None),
            P(("groups", "dp"), None),
        ),
        check_vma=False,
    )
```

profile of v0, /device:TPU:0, one launch (start us, length us, event | category | flops | bytes accessed | tf_op | source)
XLA Modules:
  0.0 196.3 jit_solution(16737418300994650969)
XLA Ops:
  4.5 24.2 %all-gather = f32[128,64,16]{1,2,0:T(8,128)S(1)} all-gather(f32[32,64,16]{1,2,0:T(8,128)S(1)} %convolution_bitcast_fusion.2), channel_id=2, replica_groups=mesh['groups'=2,'dp'=4,'tensor'=4] {'dp'}, dimensions={0}, use_global_device_ids=true | all-gather | bytes 655360 | tf_op jit(solution)/shard_map/all_gather | solution.py:13
  28.7 10.1 %all-gather.2 = f32[4,1,32]{2,1,0:T(1,128)S(1)} all-gather(f32[1,1,32]{2,1,0:T(1,128)S(1)} %bitcast.497), channel_id=1, replica_groups=mesh['groups'=2,'dp'=4,'tensor'=4] {'dp'}, dimensions={0}, use_global_device_ids=true | all-gather | bytes 640 | tf_op jit(solution)/shard_map/all_gather | solution.py:13
  38.8 3.3 %reshape.253 = bf16[2,128,32,64]{3,2,1,0:T(8,128)(2,1)S(1)} reshape(bf16[256,2048]{1,0:T(8,128)(2,1)} %param.15) | data formatting | bytes 2097152 | tf_op jit(solution)/shard_map/jvp()/reshape | solution.py:54
  42.1 2.2 %copy.210 = bf16[2,128,32,64]{1,3,2,0:T(8,128)(2,1)S(1)} copy(bf16[2,128,32,64]{3,2,1,0:T(8,128)(2,1)S(1)} %reshape.253) | data formatting | bytes 2097152
  48.4 12.4 %while.90 = (s32[]{:T(128)}, f32[32,64,16]{1,2,0:T(8,128)S(1)}, bf16[2,128,32,64]{1,3,2,0:T(8,128)(2,1)}, f32[2,32,64,16]{2,3,1,0:T(8,128)}, f32[2,128,32]{2,1,0...) while((s32[]{:T(128)}, f32[32,64,16]{1,2,0:T(8,128)S(1)}, ...), condition=%wide.region_6.7_spmd.clone, body=%wide.region_4.6_spmd.clone.sunk | while | flops 89784320 | bytes 5587197 | solution.py:59
  50.8 1.8 fusion.309
  57.0 1.8 fusion.309
  60.8 4.5 %reshape.251 = f32[2,128,32,64]{3,2,1,0:T(8,128)} reshape(bf16[256,2048]{1,0:T(8,128)(2,1)} %param.19) | data formatting | bytes 3145728 | tf_op jit(solution)/shard_map/transpose(jvp())/reshape | solution.py:60
  65.2 4.8 %copy.218 = f32[2,128,32,64]{1,3,2,0:T(8,128)} copy(f32[2,128,32,64]{3,2,1,0:T(8,128)} %reshape.251) | data formatting | bytes 4194304
  73.4 40.0 %while.91 = (s32[]{:T(128)}, f32[32,64,16]{1,2,0:T(8,128)S(1)}, f32[2,128,32,64]{1,3,2,0:T(8,128)}, f32[2,128,32]{2,1,0:T(8,128)}, f32[2,128,16]{1,2,0:T(8,128)}...) while((s32[]{:T(128)}, f32[32,64,16]{1,2,0:T(8,128)S(1)}, ...), condition=%wide.region_16.17_spmd.clone, body=%wide.region_7.16_spmd.clone.sunk | while | flops 194766816 | bytes 35066648 | solution.py:59
  81.0 1.7 fusion.332
  85.1 2.7 %fusion.331 = (f32[32,128]{1,0:T(8,128)S(1)}, f32[32,128]{1,0:T(8,128)S(1)}, f32[128,128]{1,0:T(8,128)S(1)}) fusion(f32[128,128]{1,0:T(8,128)} %fusion.330, f32[32,128]{1,0:T(8,128)} %copy.302, pred[128,128]{1,0:T(8,128)(4,1)S(1)} %iota_compare_fusion.6, bf16[128,32,64]{0,2,1:T(8,128)(2,1)S(1)} %dynamic-slice_bitcast_fusion.40, ...), kind=kOutput, calls=%fused_computation.111.clone.1 | convolution fusion | flops 71802880 | bytes 1769472 | tf_op jit(solution)/shard_map/transpose(jvp())/while/body/eval_jaxpr/checkpoint/hts,shp->thp/dot_general | solution.py:37
  105.1 2.7 %fusion.331 = (f32[32,128]{1,0:T(8,128)S(1)}, f32[32,128]{1,0:T(8,128)S(1)}, f32[128,128]{1,0:T(8,128)S(1)}) fusion(f32[128,128]{1,0:T(8,128)} %fusion.330, f32[32,128]{1,0:T(8,128)} %copy.302, pred[128,128]{1,0:T(8,128)(4,1)S(1)} %iota_compare_fusion.6, bf16[128,32,64]{0,2,1:T(8,128)(2,1)S(1)} %dynamic-slice_bitcast_fusion.40, ...), kind=kOutput, calls=%fused_computation.111.clone.1 | convolution fusion | flops 71802880 | bytes 1769472 | tf_op jit(solution)/shard_map/transpose(jvp())/while/body/eval_jaxpr/checkpoint/hts,shp->thp/dot_general | solution.py:37
  113.4 19.4 %all-gather.1 = f32[128,64,16]{1,2,0:T(8,128)S(1)} all-gather(f32[32,64,16]{1,2,0:T(8,128)S(1)} %get-tuple-element.691), channel_id=3, replica_groups=mesh['groups'=2,'dp'=4,'tensor'=4] {'dp'}, dimensions={0}, use_global_device_ids=true | all-gather | bytes 655360 | tf_op jit(solution)/shard_map/all_gather | solution.py:13
  132.9 2.7 %while.88 = (s32[]{:T(128)}, f32[32,64,16]{1,2,0:T(8,128)S(1)}, s32[]{:T(128)}, f32[4,32]{1,0:T(4,128)}, f32[4,32,64,16]{2,3,1,0:T(8,128)S(1)}, /*index=5*/s32[]{:T(128)}, s32[]{:T(128)}, s32[]{:T(128)}, s32[]{:T(128)}) while((s32[]{:T(128)}, f32[32,64,16]{1,2,0:T(8,128)S(1)}, s32[]{:T(128)}, f32[4,32]{1,0:T(4,128)}, ...), condition=%wide.region_18.19_spmd, body=%wide.region_17.18_spmd.sunk | while | flops 65542 | bytes 393747 | solution.py:22
  139.0 30.5 %while.89 = (s32[]{:T(128)}, f32[32,64,16]{1,2,0:T(8,128)S(1)}, f32[2,128,32,64]{1,3,2,0:T(8,128)}, f32[2,128,32]{2,1,0:T(8,128)}, f32[2,128,16]{1,2,0:T(8,128)}...) while((s32[]{:T(128)}, f32[32,64,16]{1,2,0:T(8,128)S(1)}, ...), condition=%wide.region_28.29_spmd, body=%wide.region_19.28_spmd.sunk | while | flops 194734048 | bytes 33165028 | solution.py:59
  142.5 2.4 %fusion.290 = (f32[32,128]{1,0:T(8,128)}, f32[32,128]{1,0:T(8,128)}, f32[128,128]{1,0:T(8,128)}) fusion(f32[128,128]{1,0:T(8,128)S(1)} %fusion.289, f32[32,128]{1,0:T(8,128)S(1)} %copy.294, pred[128,128]{1,0:T(8,128)(4,1)S(1)} %iota_compare_fusion.5, bf16[128,32,64]{0,2,1:T(8,128)(2,1)S(1)} %dynamic-slice_bitcast_fusion.33, ...), kind=kOutput, calls=%fused_computation.54.clone.1 | convolution fusion | flops 71802880 | bytes 1769472 | tf_op jit(solution)/shard_map/transpose(jvp())/while/body/eval_jaxpr/checkpoint/hts,shp->thp/dot_general | solution.py:37
  157.7 2.4 %fusion.290 = (f32[32,128]{1,0:T(8,128)}, f32[32,128]{1,0:T(8,128)}, f32[128,128]{1,0:T(8,128)}) fusion(f32[128,128]{1,0:T(8,128)S(1)} %fusion.289, f32[32,128]{1,0:T(8,128)S(1)} %copy.294, pred[128,128]{1,0:T(8,128)(4,1)S(1)} %iota_compare_fusion.5, bf16[128,32,64]{0,2,1:T(8,128)(2,1)S(1)} %dynamic-slice_bitcast_fusion.33, ...), kind=kOutput, calls=%fused_computation.54.clone.1 | convolution fusion | flops 71802880 | bytes 1769472 | tf_op jit(solution)/shard_map/transpose(jvp())/while/body/eval_jaxpr/checkpoint/hts,shp->thp/dot_general | solution.py:37
  170.3 10.9 %all-reduce.4 = (f32[256,16]{0,1:T(8,128)}, f32[256,16]{0,1:T(8,128)}) all-reduce(f32[256,16]{0,1:T(8,128)S(1)} %bitcast.492, f32[256,16]{0,1:T(8,128)S(1)} %bitcast.491), channel_id=1, replica_groups=mesh['groups'=2,'dp'=4,'tensor'=4] {'tensor'}, use_global_device_ids=true, to_apply=%region_29.30 | all-reduce | flops 8192 | bytes 65536 | tf_op jit(solution)/shard_map/psum | solution.py:104
  182.9 2.7 %add_convert_fusion = bf16[2,128,32,64]{1,3,2,0:T(8,128)(2,1)S(1)} fusion(f32[2,128,32,64]{1,3,2,0:T(8,128)} %get-tuple-element.690, f32[2,128,32,64]{1,3,2,0:T(8,128)} %get-tuple-element.693), kind=kLoop, calls=%fused_computation.160 | loop fusion | flops 1048576 | bytes 5242880 | tf_op jit(solution)/shard_map/convert_element_type | solution.py:107
  185.5 3.0 %copy.249 = bf16[2,128,32,64]{3,2,1,0:T(8,128)(2,1)S(1)} copy(bf16[2,128,32,64]{1,3,2,0:T(8,128)(2,1)S(1)} %add_convert_fusion) | data formatting | bytes 2097152
  188.5 2.4 %reshape.252 = bf16[256,2048]{1,0:T(8,128)(2,1)} reshape(bf16[2,128,32,64]{3,2,1,0:T(8,128)(2,1)S(1)} %copy.249) | data formatting | bytes 2097152
  191.0 2.9 %copy.246 = bf16[2,128,32,64]{3,2,1,0:T(8,128)(2,1)S(1)} copy(bf16[2,128,32,64]{1,3,2,0:T(8,128)(2,1)S(1)} %copy-done.19) | data formatting | bytes 2097152
  193.9 2.4 %reshape.250 = bf16[256,2048]{1,0:T(8,128)(2,1)} reshape(bf16[2,128,32,64]{3,2,1,0:T(8,128)(2,1)S(1)} %copy.246) | data formatting | bytes 2097152
  (354 shorter events, 85.5 us)
Async XLA Ops:
  0.6 44.6 %copy-start = (f32[256,16]{0,1:T(8,128)S(1)}, f32[256,16]{0,1:T(8,128)}, u32[]{:S(2)}) copy-start(f32[256,16]{0,1:T(8,128)} %param.18) | copy-start | bytes 49156
  79.2 5.8 %copy-start.40 = (f32[32]{0:T(128)}, f32[32]{0:T(128)S(1)}, u32[]{:S(2)}) copy-start(f32[32]{0:T(128)S(1)} %get-tuple-element.1405) | copy-start | bytes 388 | tf_op jit(solution)/shard_map/transpose(jvp())/while
  89.0 3.8 %copy-start.26 = (f32[2,128,32]{2,1,0:T(8,128)S(1)}, f32[2,128,32]{2,1,0:T(8,128)}, u32[]{:S(2)}) copy-start(f32[2,128,32]{2,1,0:T(8,128)} %get-tuple-element.1488) | copy-start | bytes 98308 | tf_op jit(solution)/shard_map/transpose(jvp())/while
  89.0 3.8 %copy-start.41 = (f32[32]{0:T(128)S(1)}, f32[32]{0:T(128)}, u32[]{:S(2)}) copy-start(f32[32]{0:T(128)} %copy-done.40) | copy-start | bytes 388 | tf_op jit(solution)/shard_map/transpose(jvp())/while
  89.0 3.8 %copy-start.12 = (f32[128,16]{0,1:T(8,128)S(1)}, f32[128,16]{0,1:T(8,128)}, u32[]{:S(2)}) copy-start(f32[128,16]{0,1:T(8,128)} %get-tuple-element.1396) | copy-start | bytes 24580 | tf_op jit(solution)/shard_map/transpose(jvp())/while
  89.4 4.1 %copy-start.3 = (f32[2,128,32]{2,1,0:T(8,128)S(1)}, f32[2,128,32]{2,1,0:T(8,128)}, u32[]{:S(2)}) copy-start(f32[2,128,32]{2,1,0:T(8,128)} %copy-done.2) | copy-start | bytes 98308 | tf_op jit(solution)/shard_map/transpose(jvp())/while
  99.2 5.8 %copy-start.40 = (f32[32]{0:T(128)}, f32[32]{0:T(128)S(1)}, u32[]{:S(2)}) copy-start(f32[32]{0:T(128)S(1)} %get-tuple-element.1405) | copy-start | bytes 388 | tf_op jit(solution)/shard_map/transpose(jvp())/while
  109.0 3.8 %copy-start.26 = (f32[2,128,32]{2,1,0:T(8,128)S(1)}, f32[2,128,32]{2,1,0:T(8,128)}, u32[]{:S(2)}) copy-start(f32[2,128,32]{2,1,0:T(8,128)} %get-tuple-element.1488) | copy-start | bytes 98308 | tf_op jit(solution)/shard_map/transpose(jvp())/while
  109.0 3.8 %copy-start.41 = (f32[32]{0:T(128)S(1)}, f32[32]{0:T(128)}, u32[]{:S(2)}) copy-start(f32[32]{0:T(128)} %copy-done.40) | copy-start | bytes 388 | tf_op jit(solution)/shard_map/transpose(jvp())/while
  109.0 3.8 %copy-start.12 = (f32[128,16]{0,1:T(8,128)S(1)}, f32[128,16]{0,1:T(8,128)}, u32[]{:S(2)}) copy-start(f32[128,16]{0,1:T(8,128)} %get-tuple-element.1396) | copy-start | bytes 24580 | tf_op jit(solution)/shard_map/transpose(jvp())/while
  109.4 4.1 %copy-start.3 = (f32[2,128,32]{2,1,0:T(8,128)S(1)}, f32[2,128,32]{2,1,0:T(8,128)}, u32[]{:S(2)}) copy-start(f32[2,128,32]{2,1,0:T(8,128)} %copy-done.2) | copy-start | bytes 98308 | tf_op jit(solution)/shard_map/transpose(jvp())/while
  142.5 3.8 %copy-start.18 = (f32[128,16]{0,1:T(8,128)S(1)}, f32[128,16]{0,1:T(8,128)}, u32[]{:S(2)}) copy-start(f32[128,16]{0,1:T(8,128)} %copy-done.17) | copy-start | bytes 24580 | tf_op jit(solution)/shard_map/transpose(jvp())/while
  145.0 4.0 %copy-start.14 = (f32[128,16]{0,1:T(8,128)S(1)}, f32[128,16]{0,1:T(8,128)}, u32[]{:S(2)}) copy-start(f32[128,16]{0,1:T(8,128)} %copy-done.13) | copy-start | bytes 24580 | tf_op jit(solution)/shard_map/transpose(jvp())/while
  146.5 3.6 %copy-start.22 = (f32[128,128]{1,0:T(8,128)S(1)}, f32[128,128]{1,0:T(8,128)}, u32[]{:S(2)}) copy-start(f32[128,128]{1,0:T(8,128)} %copy-done.21) | copy-start | bytes 196612 | tf_op jit(solution)/shard_map/transpose(jvp())/while
  146.5 3.6 %copy-start.31 = (f32[32,128]{1,0:T(8,128)S(1)}, f32[32,128]{1,0:T(8,128)}, u32[]{:S(2)}) copy-start(f32[32,128]{1,0:T(8,128)} %copy-done.30) | copy-start | bytes 49156 | tf_op jit(solution)/shard_map/transpose(jvp())/while
  146.6 3.6 %copy-start.34 = (pred[128,128]{1,0:T(8,128)(4,1)S(1)}, pred[128,128]{1,0:T(8,128)(4,1)}, u32[]{:S(2)}) copy-start(pred[128,128]{1,0:T(8,128)(4,1)} %copy-done.33) | copy-start | bytes 49156 | tf_op jit(solution)/shard_map/transpose(jvp())/while
  150.2 4.1 %copy-start.5 = (f32[2,128,32]{2,1,0:T(8,128)S(1)}, f32[2,128,32]{2,1,0:T(8,128)}, u32[]{:S(2)}) copy-start(f32[2,128,32]{2,1,0:T(8,128)} %copy-done.4) | copy-start | bytes 98308 | tf_op jit(solution)/shard_map/transpose(jvp())/while
  157.7 3.8 %copy-start.18 = (f32[128,16]{0,1:T(8,128)S(1)}, f32[128,16]{0,1:T(8,128)}, u32[]{:S(2)}) copy-start(f32[128,16]{0,1:T(8,128)} %copy-done.17) | copy-start | bytes 24580 | tf_op jit(solution)/shard_map/transpose(jvp())/while
  160.2 4.0 %copy-start.14 = (f32[128,16]{0,1:T(8,128)S(1)}, f32[128,16]{0,1:T(8,128)}, u32[]{:S(2)}) copy-start(f32[128,16]{0,1:T(8,128)} %copy-done.13) | copy-start | bytes 24580 | tf_op jit(solution)/shard_map/transpose(jvp())/while
  161.8 3.6 %copy-start.22 = (f32[128,128]{1,0:T(8,128)S(1)}, f32[128,128]{1,0:T(8,128)}, u32[]{:S(2)}) copy-start(f32[128,128]{1,0:T(8,128)} %copy-done.21) | copy-start | bytes 196612 | tf_op jit(solution)/shard_map/transpose(jvp())/while
  161.8 3.6 %copy-start.31 = (f32[32,128]{1,0:T(8,128)S(1)}, f32[32,128]{1,0:T(8,128)}, u32[]{:S(2)}) copy-start(f32[32,128]{1,0:T(8,128)} %copy-done.30) | copy-start | bytes 49156 | tf_op jit(solution)/shard_map/transpose(jvp())/while
  161.8 3.6 %copy-start.34 = (pred[128,128]{1,0:T(8,128)(4,1)S(1)}, pred[128,128]{1,0:T(8,128)(4,1)}, u32[]{:S(2)}) copy-start(pred[128,128]{1,0:T(8,128)(4,1)} %copy-done.33) | copy-start | bytes 49156 | tf_op jit(solution)/shard_map/transpose(jvp())/while
  165.3 3.5 %copy-start.15 = (f32[128,16]{0,1:T(8,128)S(1)}, f32[128,16]{0,1:T(8,128)}, u32[]{:S(2)}) copy-start(f32[128,16]{0,1:T(8,128)} %copy-done.13) | copy-start | bytes 24580 | tf_op jit(solution)/shard_map/transpose(jvp())/while
  165.4 4.1 %copy-start.5 = (f32[2,128,32]{2,1,0:T(8,128)S(1)}, f32[2,128,32]{2,1,0:T(8,128)}, u32[]{:S(2)}) copy-start(f32[2,128,32]{2,1,0:T(8,128)} %copy-done.4) | copy-start | bytes 98308 | tf_op jit(solution)/shard_map/transpose(jvp())/while
  (62 other events, 149.0 us)
where the time goes:
time: 198 us; the launch traced here: 196 us
  local copies, waits for them, and re-layouts  65.2 us (33%)
  blocking collectives  64.6 us (33%)
  matrix products  42.4 us (21%)
  other arithmetic  21.8 us (11%)
    all_gather x3, blocking collectives, carried_in(): gathered = jax.tree.map(lambda a: lax.all_gather(a, axis), part)  53.7 us
    unnamed x18, local copies, waits for them, and re-layouts  22 us
    dot_general x10, matrix products, block_pass(): jnp.einsum('hts,shp->thp', mixing, inputs, preferred_element_type=jnp.flo...  17.3 us
    squeeze x24, local copies, waits for them, and re-layouts, run_rows(): lax.scan(jax.checkpoint(block_pass), carry_state, pieces)  12 us
    psum x1, blocking collectives, local(): shared_in, shared_out = lax.psum((gradients[2], gradients[3]), 'tensor')  10.9 us
    dot_general x14, matrix products, block_pass(): jnp.einsum('tn,hpn->thp', out_rows, carry_state, preferred_element_type=j...  10.3 us
    dot_general x14, matrix products, block_pass(): jnp.dot(out_rows, in_rows.T, preferred_element_type=jnp.float32, precisio...  9.72 us
    another operation x14, other arithmetic, block_pass(): cumulative = jnp.cumsum(decays, axis=0)  9.33 us

commit v1 on v0

v1 whole, which is shorter than its diff:
```python
import functools

import jax
import jax.numpy as jnp
from jax import lax
from jax.experimental import pallas as pl
from jax.experimental.pallas import tpu as pltpu
from jax.sharding import PartitionSpec as P

F32 = jnp.float32
BF16 = jnp.bfloat16
L = 128
PIECES = 4
MESH = pl.DeviceIdType.MESH
HI = lax.Precision.HIGHEST
NN = (((1,), (0,)), ((), ()))
NT = (((1,), (1,)), ((), ()))
TN = (((0,), (0,)), ((), ()))


def dot(a, b, dims=NN, precision=None):
    return lax.dot_general(a, b, dims, precision=precision, preferred_element_type=F32)


def split(a, terms):
    parts = []
    for _ in range(terms):
        part = a.astype(BF16)
        parts.append(part)
        a = a - part.astype(F32)
    return parts


def exact_right(a, ones, dims=NN, terms=3):
    return sum(dot(part, ones, dims) for part in split(a, terms))


def exact_left(ones, a, dims=NN, terms=3):
    return sum(dot(ones, part, dims) for part in split(a, terms))


def iota(shape, dim):
    return lax.broadcasted_iota(jnp.int32, shape, dim)


def ones_where(cond):
    return jnp.where(cond, 1.0, 0.0).astype(BF16)


def kernel(
    hops, peers, heads, x_ref, ld_ref, b_ref, c_ref, g_ref,
    y_ref, dx_ref, gd_ref, d_in_ref, d_out_ref,
    ys, dxs, own, gown, fin, fout, gin, gout, sbd, gbd, pex, mall,
    fsend, frecv, bsend, brecv, msend, mrecv,
):
    rows, width = x_ref.shape
    state = b_ref.shape[0]
    head = width // heads
    chunks = rows // L
    per = heads // PIECES
    wide = per * head
    place = lax.axis_index("dp")
    mine = lax.axis_index("tensor")

    barrier = pltpu.get_barrier_semaphore()
    for d in range(1, peers):
        pl.semaphore_signal(
            barrier, inc=1, device_id={"tensor": lax.rem(mine + d, peers)}, device_id_type=MESH
        )

    @pl.when(place > 0)
    def _():
        pl.semaphore_signal(barrier, inc=1, device_id={"dp": place - 1}, device_id_type=MESH)

    @pl.when(place < hops - 1)
    def _():
        pl.semaphore_signal(barrier, inc=1, device_id={"dp": place + 1}, device_id_type=MESH)

    causal = iota((L, L), 0) >= iota((L, L), 1)
    tril = ones_where(causal)
    upper = ones_where(iota((L, L), 0) <= iota((L, L), 1))
    by_col = ones_where(iota((heads, width), 0) == iota((heads, width), 1) // head)
    by_state = ones_where(iota((heads, heads * state), 0) == iota((heads, heads * state), 1) // state)
    tile = ones_where(iota((state, per * state), 0) == iota((state, per * state), 1) % state)
    quad = 4 * head

    cum, cum_t, e_exp, t_exp, ce, be, b_t, c_t = [], [], [], [], [], [], [], []
    for c in range(chunks):
        at = pl.ds(c * L, L)
        cu = exact_left(tril, ld_ref[:, at], NT)
        cut = exact_right(ld_ref[:, at], upper)
        cum.append(cu)
        cum_t.append(cut)
        bt = b_ref[:, at]
        ct = c_ref[:, at]
        b_t.append(bt)
        c_t.append(ct)
        pex[c] = jnp.exp(exact_right(cu[L - 8:, :], by_col))
        et = jnp.exp(cut)
        tt = jnp.exp(cut[:, L - 1:] - cut)
        for k in range(width // quad):
            lanes = pl.ds(k * quad, quad)
            lhs_b = jnp.concatenate([bt * tt[h:h + 1, :] for h in range(4 * k, 4 * k + 4)], 0).astype(BF16)
            lhs_c = jnp.concatenate([ct * et[h:h + 1, :] for h in range(4 * k, 4 * k + 4)], 0).astype(BF16)
            rb = dot(lhs_b, x_ref[at, lanes])
            rc = dot(lhs_c, g_ref[at, lanes])
            which = iota((state, quad), 1) // head
            ob = rb[:state]
            oc = rc[:state]
            for h in range(1, 4):
                ob = jnp.where(which == h, rb[h * state:(h + 1) * state], ob)
                oc = jnp.where(which == h, rc[h * state:(h + 1) * state], oc)
            own[c, k * quad // wide, :, (k * quad) % wide:(k * quad) % wide + quad] = ob
            gown[c, k * quad // wide, :, (k * quad) % wide:(k * quad) % wide + quad] = oc

    pl.semaphore_wait(
        barrier, peers - 1 + jnp.minimum(place, 1) + jnp.minimum(hops - 1 - place, 1)
    )

    def decay(c, k):
        return pex[c, 7:8, k * wide:(k + 1) * wide]

    def f_copy(k):
        return pltpu.make_async_remote_copy(
            src_ref=fout.at[k], dst_ref=fin.at[k], send_sem=fsend.at[k], recv_sem=frecv.at[k],
            device_id={"dp": place + 1}, device_id_type=MESH,
        )

    def b_copy(k):
        return pltpu.make_async_remote_copy(
            src_ref=gout.at[k], dst_ref=gin.at[k], send_sem=bsend.at[k], recv_sem=brecv.at[k],
            device_id={"dp": place - 1}, device_id_type=MESH,
        )

    def relay(first):
        for k in range(PIECES):
            @pl.when(place == 0 if first else place > 0)
            def _():
                if first:
                    fin[k] = jnp.zeros(fin.shape[1:], F32)
                else:
                    f_copy(k).wait_recv()

            @pl.when(place < hops - 1)
            def _():
                s = own[0, k] if first else decay(0, k) * fin[k] + own[0, k]
                for c in range(1, chunks):
                    s = decay(c, k) * s + own[c, k]
                fout[k] = s
                f_copy(k).start()

    def relay_back(first):
        for k in range(PIECES):
            @pl.when(place == hops - 1 if first else place < hops - 1)
            def _():
                if first:
                    gin[k] = jnp.zeros(gin.shape[1:], F32)
                else:
                    b_copy(k).wait_recv()

            @pl.when(place > 0)
            def _():
                last = chunks - 1
                s = gown[last, k] if first else decay(last, k) * gin[k] + gown[last, k]
                for c in range(chunks - 2, -1, -1):
                    s = decay(c, k) * s + gown[c, k]
                gout[k] = s
                b_copy(k).start()

    stages = min(hops, 4)
    from_end = hops - 1 - place

    def exchange(stage):
        when = (lambda v: v >= stage) if stage == stages - 1 else (lambda v: v == stage)

        @pl.when(when(place))
        def _():
            relay(stage == 0)

        @pl.when(when(from_end))
        def _():
            relay_back(stage == 0)

    exchange(0)

    scores, grad_scores = [], []
    for c in range(chunks):
        at = pl.ds(c * L, L)
        s = dot(c_t[c], b_t[c], TN, HI)
        scores.append(jnp.where(causal, s, 0.0))
        grad_scores.append(jnp.zeros((L, L), F32))
        ct8 = exact_right(c_t[c], tile, TN)
        bt8 = exact_right(b_t[c], tile, TN)
        cue = exact_right(cum[c], by_state)
        ee = jnp.exp(cue)
        te = jnp.exp(cue[L - 1:, :] - cue)
        e_exp.append(ee)
        t_exp.append(te)
        lanes = per * state
        ce.append([(ct8 * ee[:, k * lanes:(k + 1) * lanes]).astype(BF16) for k in range(PIECES)])
        be.append([(bt8 * te[:, k * lanes:(k + 1) * lanes]).astype(BF16) for k in range(PIECES)])

    pair = 2 * head
    left = ones_where(iota((L, pair), 1) < head)
    right = ones_where(iota((L, pair), 1) >= head)
    units = [(c, p) for p in range(width // pair) for c in range(chunks)]
    for n, (c, p) in enumerate(units):
        for stage in range(1, stages):
            if n == len(units) * stage // (stages - 1) - 1 and stage < stages - 1:
                exchange(stage)
        at = pl.ds(c * L, L)
        lanes = pl.ds(p * pair, pair)
        weights = []
        for h in (2 * p, 2 * p + 1):
            diff = cum[c][:, h:h + 1] - cum_t[c][h:h + 1, :]
            weights.append(jnp.exp(jnp.minimum(diff, 0.0)))
        mix = [(w * scores[c]).astype(BF16) for w in weights]
        x = x_ref[at, lanes]
        g = g_ref[at, lanes]
        x2 = jnp.concatenate([x * left, x * right], 0)
        g2 = jnp.concatenate([g * left, g * right], 0)
        ys[at, lanes] = dot(jnp.concatenate(mix, 1), x2)
        dxs[at, lanes] = dot(jnp.concatenate(mix, 0), g2, TN)
        dm = dot(g, x2, NT)
        grad_scores[c] += weights[0] * dm[:, :L] + weights[1] * dm[:, L:]
    if stages > 1:
        exchange(stages - 1)

    block = ones_where(iota((per * state, wide), 0) // state == iota((per * state, wide), 1) // head)
    acc_c = [jnp.zeros((L, per * state), F32) for _ in range(chunks)]
    acc_b = [jnp.zeros((L, per * state), F32) for _ in range(chunks)]
    ends = []
    for k in range(PIECES):
        states = [fin[k]]
        for c in range(chunks):
            states.append(decay(c, k) * states[c] + own[c, k])
        grads = [gin[k]]
        for c in range(chunks - 1, 0, -1):
            grads.append(decay(c, k) * grads[-1] + gown[c, k])
        grads = grads[::-1]
        ends.append([jnp.sum(grads[c] * states[c + 1], 0, keepdims=True) for c in range(chunks)])
        for c in range(chunks):
            at = pl.ds(c * L, L)
            cols = pl.ds(k * wide, wide)
            lanes = slice(k * per * state, (k + 1) * per * state)
            s2 = jnp.concatenate([states[c].astype(BF16)] * per, 0) * block
            r2 = jnp.concatenate([grads[c].astype(BF16)] * per, 0) * block
            sbd[c, k] = s2
            gbd[c, k] = r2
            acc_c[c] += dot(g_ref[at, cols], s2, NT) * e_exp[c][:, lanes]
            acc_b[c] += dot(x_ref[at, cols], r2, NT) * t_exp[c][:, lanes]

    for c in range(chunks):
        ds = jnp.where(causal, grad_scores[c], 0.0)
        mall[mine, :state, c * L:(c + 1) * L] = exact_left(tile, acc_c[c], NT) + dot(b_t[c], ds, NT, HI)
        mall[mine, state:, c * L:(c + 1) * L] = exact_left(tile, acc_b[c], NT) + dot(c_t[c], ds, NN, HI)

    def m_copy(d, slot):
        return pltpu.make_async_remote_copy(
            src_ref=mall.at[mine], dst_ref=mall.at[slot], send_sem=msend.at[d - 1], recv_sem=mrecv.at[d - 1],
            device_id={"tensor": lax.rem(mine + d, peers)}, device_id_type=MESH,
        )

    for d in range(1, peers):
        m_copy(d, mine).start()

    for c in range(chunks):
        at = pl.ds(c * L, L)
        dcum = jnp.zeros((heads, L), F32)
        for k in range(PIECES):
            cols = pl.ds(k * wide, wide)
            y = ys[at, cols] + dot(ce[c][k], sbd[c, k])
            dx = dxs[at, cols] + dot(be[c][k], gbd[c, k])
            y_ref[at, cols] = y.astype(BF16)
            dx_ref[at, cols] = dx.astype(BF16)
            q = g_ref[at, cols].astype(F32) * y - x_ref[at, cols].astype(F32) * dx
            q += jnp.where(iota((L, wide), 0) == L - 1, ends[k][c], 0.0)
            dcum += exact_left(by_col[:, k * wide:(k + 1) * wide], q, NT, 2)
        gd_ref[:, at] = exact_right(dcum, tril)

    for d in range(1, peers):
        m_copy(d, lax.rem(mine + peers - d, peers)).wait_recv()
        m_copy(d, mine).wait_send()
    total = mall[0]
    for d in range(1, peers):
        total += mall[d]
    d_out_ref[...] = total[:state]
    d_in_ref[...] = total[state:]

    @pl.when(place < hops - 1)
    def _():
        for k in range(PIECES):
            f_copy(k).wait_send()

    @pl.when(place > 0)
    def _():
        for k in range(PIECES):
            b_copy(k).wait_send()


def local(hops, peers, x_inner, log_decay, in_map, out_map, grad_out):
    rows, width = x_inner.shape
    heads = log_decay.shape[1]
    state = in_map.shape[1]
    chunks = rows // L
    wide = width // PIECES
    piece = (PIECES, state, wide)
    vm = pl.BlockSpec(memory_space=pltpu.VMEM)
    y, dx, gd, d_in, d_out = pl.pallas_call(
        functools.partial(kernel, hops, peers, heads),
        out_shape=(
            jax.ShapeDtypeStruct((rows, width), BF16),
            jax.ShapeDtypeStruct((rows, width), BF16),
            jax.ShapeDtypeStruct((heads, rows), F32),
            jax.ShapeDtypeStruct((state, rows), F32),
            jax.ShapeDtypeStruct((state, rows), F32),
        ),
        in_specs=[vm] * 5,
        out_specs=(vm,) * 5,
        scratch_shapes=[
            pltpu.VMEM((rows, width), F32),
            pltpu.VMEM((rows, width), F32),
            pltpu.VMEM((chunks,) + piece, F32),
            pltpu.VMEM((chunks,) + piece, F32),
            pltpu.VMEM(piece, F32),
            pltpu.VMEM(piece, F32),
            pltpu.VMEM(piece, F32),
            pltpu.VMEM(piece, F32),
            pltpu.VMEM((chunks, PIECES, heads // PIECES * state, wide), BF16),
            pltpu.VMEM((chunks, PIECES, heads // PIECES * state, wide), BF16),
            pltpu.VMEM((chunks, 8, width), F32),
            pltpu.VMEM((peers, 2 * state, rows), F32),
            pltpu.SemaphoreType.DMA((PIECES,)),
            pltpu.SemaphoreType.DMA((PIECES,)),
            pltpu.SemaphoreType.DMA((PIECES,)),
            pltpu.SemaphoreType.DMA((PIECES,)),
            pltpu.SemaphoreType.DMA((peers - 1,)),
            pltpu.SemaphoreType.DMA((peers - 1,)),
        ],
        compiler_params=pltpu.CompilerParams(
            collective_id=0, has_side_effects=True, vmem_limit_bytes=40 * 2**20
        ),
    )(x_inner, log_decay.T, in_map.T, out_map.T, grad_out)
    return y, dx, gd.T, d_in.T, d_out.T


def solution(mesh):
    row = ("groups", "dp")
    placed = (P(row, "tensor"), P(row, "tensor"), P(row, None), P(row, None), P(row, "tensor"))
    return jax.shard_map(
        functools.partial(local, mesh.shape["dp"], mesh.shape["tensor"]),
        mesh=mesh,
        in_specs=placed,
        out_specs=(P(row, "tensor"), P(row, "tensor"), P(row, "tensor"), P(row, None), P(row, None)),
        check_vma=False,
    )
```

time: 198 us -> 28.7 us (0.14)
  blocking collectives: 64.6 us -> 0 us
  local copies, waits for them, and re-layouts: 65.2 us -> 8.4 us
  matrix products: 42.4 us -> 0 us
  other arithmetic: 21.8 us -> 0 us
  Pallas kernels: 0 us -> 19.3 us
    all_gather x3 -> x0, blocking collectives: 53.7 us -> none  [carried_in(): gathered = jax.tree.map(lambda a: lax.all_gather(a, axis), part)]
    dot_general x49 -> x0, matrix products: 42.4 us -> none  [the longest x10 17.3 us: block_pass(): jnp.einsum('hts,shp->thp', mixing, inputs, preferred_element_type=jnp.flo...]
    pallas_call x0 -> x1, Pallas kernels: none -> 19.3 us  [local(): pl.pallas_call(functools.partial(kernel, hops, peers, heads), out_shape=(...]
    unnamed x18 -> x15, local copies, waits for them, and re-layouts: 22 us -> 8.4 us
    squeeze x26 -> x0, local copies, waits for them, and re-layouts: 12 us -> none  [the longest x24 12 us: run_rows(): lax.scan(jax.checkpoint(block_pass), carry_state, pieces)]
    psum x1 -> x0, blocking collectives: 10.9 us -> none  [local(): shared_in, shared_out = lax.psum((gradients[2], gradients[3]), 'tensor')]
    reshape x7 -> x0, local copies, waits for them, and re-layouts: 10.2 us -> none  [the longest x1 4.48 us: run_rows(): return (outputs.reshape(row_count, head_count * head_width), last_state)]
    another operation x19 -> x0, other arithmetic: 10.1 us -> none  [the longest x14 9.33 us: block_pass(): cumulative = jnp.cumsum(decays, axis=0)]
where the time goes in v1:
time: 28.7 us; the launch traced here: 28.3 us
  Pallas kernels  19.3 us (67%)
  local copies, waits for them, and re-layouts  8.4 us (29%)
  between operations  0.66 us (2%)
    pallas_call x1, Pallas kernels, local(): pl.pallas_call(functools.partial(kernel, hops, peers, heads), out_shape=(...  19.3 us
    unnamed x15, local copies, waits for them, and re-layouts  8.4 us

profile of v1, /device:TPU:0, one launch (start us, length us, event | category | flops | bytes accessed | tf_op | source)
XLA Modules:
  0.0 28.3 jit_solution(17389126532950888309)
XLA Ops:
  0.6 0.0 copy-start
  0.6 1.2 %copy-done = bf16[256,2048]{1,0:T(8,128)(2,1)S(1)} copy-done((bf16[256,2048]{1,0:T(8,128)(2,1)S(1)}, bf16[256,2048]{1,0:T(8,128)(2,1)}, u32[]{:S(2)}) %copy-start) | copy-done | bytes 1048600
  1.9 0.0 copy-start.1
  1.9 1.2 %copy-done.1 = bf16[256,2048]{1,0:T(8,128)(2,1)S(1)} copy-done((bf16[256,2048]{1,0:T(8,128)(2,1)S(1)}, bf16[256,2048]{1,0:T(8,128)(2,1)}, u32[]{:S(2)}) %copy-start.1) | copy-done | bytes 1048600
  3.1 0.0 copy-start.2
  3.1 0.8 %copy-done.2 = f32[256,32]{0,1:T(8,128)S(1)} copy-done((f32[256,32]{0,1:T(8,128)S(1)}, f32[256,32]{0,1:T(8,128)}, u32[]{:S(2)}) %copy-start.2) | copy-done | bytes 32792
  3.8 0.0 copy-start.3
  3.8 0.7 %copy-done.3 = f32[256,16]{0,1:T(8,128)S(1)} copy-done((f32[256,16]{0,1:T(8,128)S(1)}, f32[256,16]{0,1:T(8,128)}, u32[]{:S(2)}) %copy-start.3) | copy-done | bytes 16408
  4.6 0.0 copy-start.4
  4.6 0.7 %copy-done.4 = f32[256,16]{0,1:T(8,128)S(1)} copy-done((f32[256,16]{0,1:T(8,128)S(1)}, f32[256,16]{0,1:T(8,128)}, u32[]{:S(2)}) %copy-start.4) | copy-done | bytes 16408
  5.3 19.3 %shard_map.92 = (bf16[256,2048]{1,0:T(8,128)(2,1)S(1)}, bf16[256,2048]{1,0:T(8,128)(2,1)S(1)}, f32[32,256]{1,0:T(8,128)S(1)}, f32[16,256]{1,0:T(8,128)S(1)}, f32[16,256]{1,0:T(8,128)S(1)}) custom-call(bf16[256,2048]{1,0:T(8,128)(2,1)S(1)} %copy-done, f32[32,256]{1,0:T(8,128)S(1)} %bitcast.6, f32[16,256]{1,0:T(8,128)S(1)} %bitcast.8, f32[16,256]{1,0:T(8,128)S(1)} %bitcast.9, ...), custom_call_target="tpu_custom_call" | custom-call | tf_op jit(solution)/shard_map/pallas_call | solution.py:309
  24.6 1.0 %copy.15 = bf16[256,2048]{1,0:T(8,128)(2,1)} copy(bf16[256,2048]{1,0:T(8,128)(2,1)S(1)} %get-tuple-element.20) | data formatting | bytes 2097152
  25.5 1.0 %copy.16 = bf16[256,2048]{1,0:T(8,128)(2,1)} copy(bf16[256,2048]{1,0:T(8,128)(2,1)S(1)} %get-tuple-element.21) | data formatting | bytes 2097152
  26.5 0.6 %copy.17 = f32[256,32]{0,1:T(8,128)} copy(f32[256,32]{0,1:T(8,128)S(1)} %bitcast.7) | data formatting | bytes 65536
  27.1 0.6 %copy.18 = f32[256,16]{0,1:T(8,128)} copy(f32[256,16]{0,1:T(8,128)S(1)} %bitcast.11) | data formatting | bytes 32768
  27.7 0.6 %copy.19 = f32[256,16]{0,1:T(8,128)} copy(f32[256,16]{0,1:T(8,128)S(1)} %bitcast.10) | data formatting | bytes 32768
Async XLA Ops:
  0.6 1.2 %copy-start = (bf16[256,2048]{1,0:T(8,128)(2,1)S(1)}, bf16[256,2048]{1,0:T(8,128)(2,1)}, u32[]{:S(2)}) copy-start(bf16[256,2048]{1,0:T(8,128)(2,1)} %x_ref.1) | copy-start | bytes 3145732
  1.9 1.2 %copy-start.1 = (bf16[256,2048]{1,0:T(8,128)(2,1)S(1)}, bf16[256,2048]{1,0:T(8,128)(2,1)}, u32[]{:S(2)}) copy-start(bf16[256,2048]{1,0:T(8,128)(2,1)} %g_ref.1) | copy-start | bytes 3145732
  3.1 0.8 %copy-start.2 = (f32[256,32]{0,1:T(8,128)S(1)}, f32[256,32]{0,1:T(8,128)}, u32[]{:S(2)}) copy-start(f32[256,32]{0,1:T(8,128)} %param.6) | copy-start | bytes 98308
  3.8 0.7 %copy-start.3 = (f32[256,16]{0,1:T(8,128)S(1)}, f32[256,16]{0,1:T(8,128)}, u32[]{:S(2)}) copy-start(f32[256,16]{0,1:T(8,128)} %param.7) | copy-start | bytes 49156
  4.6 0.7 %copy-start.4 = (f32[256,16]{0,1:T(8,128)S(1)}, f32[256,16]{0,1:T(8,128)}, u32[]{:S(2)}) copy-start(f32[256,16]{0,1:T(8,128)} %param.8) | copy-start | bytes 49156

commit v2 on v1

--- a/solution.py
+++ b/solution.py
@@ -48,8 +48,9 @@
 
 
 def kernel(
-    hops, peers, heads, x_ref, ld_ref, b_ref, c_ref, g_ref,
-    y_ref, dx_ref, gd_ref, d_in_ref, d_out_ref,
+    hops, peers, heads, x_hbm, ld_hbm, b_hbm, c_hbm, g_hbm,
+    yz_ref, small_ref,
+    x_ref, ld_ref, b_ref, c_ref, g_ref, load,
     ys, dxs, own, gown, fin, fout, gin, gout, sbd, gbd, pex, mall,
     fsend, frecv, bsend, brecv, msend, mrecv,
 ):
@@ -59,6 +60,14 @@
     chunks = rows // L
     per = heads // PIECES
     wide = per * head
+    loads = [
+        pltpu.make_async_copy(src, dst, load.at[i])
+        for i, (src, dst) in enumerate(
+            [(ld_hbm, ld_ref), (b_hbm, b_ref), (c_hbm, c_ref), (x_hbm, x_ref), (g_hbm, g_ref)]
+        )
+    ]
+    for copy in loads:
+        copy.start()
     place = lax.axis_index("dp")
     mine = lax.axis_index("tensor")
 
@@ -84,6 +93,8 @@
     tile = ones_where(iota((state, per * state), 0) == iota((state, per * state), 1) % state)
     quad = 4 * head
 
+    for copy in loads:
+        copy.wait()
     cum, cum_t, e_exp, t_exp, ce, be, b_t, c_t = [], [], [], [], [], [], [], []
     for c in range(chunks):
         at = pl.ds(c * L, L)
@@ -271,12 +282,12 @@
             cols = pl.ds(k * wide, wide)
             y = ys[at, cols] + dot(ce[c][k], sbd[c, k])
             dx = dxs[at, cols] + dot(be[c][k], gbd[c, k])
-            y_ref[at, cols] = y.astype(BF16)
-            dx_ref[at, cols] = dx.astype(BF16)
+            yz_ref[0, at, cols] = y.astype(BF16)
+            yz_ref[1, at, cols] = dx.astype(BF16)
             q = g_ref[at, cols].astype(F32) * y - x_ref[at, cols].astype(F32) * dx
             q += jnp.where(iota((L, wide), 0) == L - 1, ends[k][c], 0.0)
             dcum += exact_left(by_col[:, k * wide:(k + 1) * wide], q, NT, 2)
-        gd_ref[:, at] = exact_right(dcum, tril)
+        small_ref[2 * state:, at] = exact_right(dcum, tril)
 
     for d in range(1, peers):
         m_copy(d, lax.rem(mine + peers - d, peers)).wait_recv()
@@ -284,8 +295,7 @@
     total = mall[0]
     for d in range(1, peers):
         total += mall[d]
-    d_out_ref[...] = total[:state]
-    d_in_ref[...] = total[state:]
+    small_ref[:2 * state] = total
 
     @pl.when(place < hops - 1)
     def _():
@@ -306,18 +316,21 @@
     wide = width // PIECES
     piece = (PIECES, state, wide)
     vm = pl.BlockSpec(memory_space=pltpu.VMEM)
-    y, dx, gd, d_in, d_out = pl.pallas_call(
+    yz, small = pl.pallas_call(
         functools.partial(kernel, hops, peers, heads),
         out_shape=(
-            jax.ShapeDtypeStruct((rows, width), BF16),
-            jax.ShapeDtypeStruct((rows, width), BF16),
-            jax.ShapeDtypeStruct((heads, rows), F32),
-            jax.ShapeDtypeStruct((state, rows), F32),
-            jax.ShapeDtypeStruct((state, rows), F32),
+            jax.ShapeDtypeStruct((2, rows, width), BF16),
+            jax.ShapeDtypeStruct((2 * state + heads, rows), F32),
         ),
-        in_specs=[vm] * 5,
-        out_specs=(vm,) * 5,
+        in_specs=[pl.BlockSpec(memory_space=pltpu.HBM)] * 5,
+        out_specs=(vm,) * 2,
         scratch_shapes=[
+            pltpu.VMEM((rows, width), BF16),
+            pltpu.VMEM((heads, rows), F32),
+            pltpu.VMEM((state, rows), F32),
+            pltpu.VMEM((state, rows), F32),
+            pltpu.VMEM((rows, width), BF16),
+            pltpu.SemaphoreType.DMA((5,)),
             pltpu.VMEM((rows, width), F32),
             pltpu.VMEM((rows, width), F32),
             pltpu.VMEM((chunks,) + piece, F32),
@@ -340,8 +353,8 @@
         compiler_params=pltpu.CompilerParams(
             collective_id=0, has_side_effects=True, vmem_limit_bytes=40 * 2**20
         ),
-    )(x_inner, log_decay.T, in_map.T, out_map.T, grad_out)
-    return y, dx, gd.T, d_in.T, d_out.T
+    )(*[pltpu.with_memory_space_constraint(a, pltpu.HBM) for a in (x_inner, log_decay.T, in_map.T, out_map.T, grad_out)])
+    return yz[0], yz[1], small[2 * state:].T, small[state:2 * state].T, small[:state].T
 
 
 def solution(mesh):

time: 28.7 us -> 24.5 us (0.85)
  local copies, waits for them, and re-layouts: 8.4 us -> 2.8 us
  Pallas kernels: 19.3 us -> 20.9 us
    unnamed x15 -> x0, local copies, waits for them, and re-layouts: 8.4 us -> none
    pallas_call x1, Pallas kernels: 19.3 us -> 20.9 us  [local(): pl.pallas_call(functools.partial(kernel, hops, peers, heads), out_shape=(...]
    squeeze x0 -> x1, local copies, waits for them, and re-layouts: none -> 1.57 us  [local(): yz[1]]
    transpose x0 -> x2, local copies, waits for them, and re-layouts: none -> 1.23 us  [the longest x1 0.62 us: local(): small[2 * state:]]
where the time goes in v2:
time: 24.5 us; the launch traced here: 24.4 us
  Pallas kernels  20.9 us (85%)
  local copies, waits for them, and re-layouts  2.8 us (11%)
  between operations  0.64 us (3%)
    pallas_call x1, Pallas kernels, local(): pl.pallas_call(functools.partial(kernel, hops, peers, heads), out_shape=(...  20.9 us
    squeeze x1, local copies, waits for them, and re-layouts, local(): yz[1]  1.57 us
    transpose x1, local copies, waits for them, and re-layouts, local(): small[2 * state:]  0.62 us
    transpose x1, local copies, waits for them, and re-layouts, local(): small[:state]  0.61 us

profile of v2, /device:TPU:0, one launch (start us, length us, event | category | flops | bytes accessed | tf_op | source)
XLA Modules:
  0.0 24.4 jit_solution(11130099507767940176)
XLA Ops:
  0.6 20.9 %shard_map.92 = (bf16[2,256,2048]{2,1,0:T(8,128)(2,1)S(1)}, f32[64,256]{1,0:T(8,128)S(1)}) custom-call(bf16[256,2048]{1,0:T(8,128)(2,1)} %x_hbm.1, f32[32,256]{1,0:T(8,128)} %bitcast.13, f32[16,256]{1,0:T(8,128)} %bitcast.14, f32[16,256]{1,0:T(8,128)} %bitcast.15, bf16[256,2048]{1,0:T(8,128)(2,1)} %g_hbm.1), custom_call_target="tpu_custom_call" | custom-call | tf_op jit(solution)/shard_map/pallas_call | solution.py:319
  21.6 1.6 %slice_bitcast_fusion = (bf16[256,2048]{1,0:T(8,128)(2,1)}, bf16[256,2048]{1,0:T(8,128)(2,1)}) fusion(bf16[2,256,2048]{2,1,0:T(8,128)(2,1)S(1)} %get-tuple-element.7), kind=kLoop, calls=%fused_computation | loop fusion | bytes 4194304 | tf_op jit(solution)/shard_map/squeeze | solution.py:357
  23.1 0.6 %slice_bitcast_fusion.2 = f32[256,32]{0,1:T(8,128)} fusion(f32[64,256]{1,0:T(8,128)S(1)} %get-tuple-element.8), kind=kLoop, calls=%fused_computation.2 | loop fusion | bytes 65536 | tf_op jit(solution)/shard_map/transpose | solution.py:357
  23.8 0.6 %slice_bitcast_fusion.3 = (f32[256,16]{0,1:T(8,128)}, f32[256,16]{0,1:T(8,128)}) fusion(f32[64,256]{1,0:T(8,128)S(1)} %get-tuple-element.8), kind=kLoop, calls=%fused_computation.3 | loop fusion | bytes 65536 | tf_op jit(solution)/shard_map/transpose | solution.py:357

commit v3 on v2

--- a/solution.py
+++ b/solution.py
@@ -53,6 +53,7 @@
     x_ref, ld_ref, b_ref, c_ref, g_ref, load,
     ys, dxs, own, gown, fin, fout, gin, gout, sbd, gbd, pex, mall,
     fsend, frecv, bsend, brecv, msend, mrecv,
+    ffar, ffar_in, bfar, bfar_in, fsend2, frecv2, bsend2, brecv2,
 ):
     rows, width = x_ref.shape
     state = b_ref.shape[0]
@@ -77,13 +78,23 @@
             barrier, inc=1, device_id={"tensor": lax.rem(mine + d, peers)}, device_id_type=MESH
         )
 
-    @pl.when(place > 0)
-    def _():
-        pl.semaphore_signal(barrier, inc=1, device_id={"dp": place - 1}, device_id_type=MESH)
-
-    @pl.when(place < hops - 1)
-    def _():
-        pl.semaphore_signal(barrier, inc=1, device_id={"dp": place + 1}, device_id_type=MESH)
+    short = hops == 4
+    if short:
+        for d in range(1, hops):
+            pl.semaphore_signal(
+                barrier, inc=1, device_id={"dp": lax.rem(place + d, hops)}, device_id_type=MESH
+            )
+        near = hops - 1
+    else:
+        near = jnp.minimum(place, 1) + jnp.minimum(hops - 1 - place, 1)
+
+        @pl.when(place > 0)
+        def _():
+            pl.semaphore_signal(barrier, inc=1, device_id={"dp": place - 1}, device_id_type=MESH)
+
+        @pl.when(place < hops - 1)
+        def _():
+            pl.semaphore_signal(barrier, inc=1, device_id={"dp": place + 1}, device_id_type=MESH)
 
     causal = iota((L, L), 0) >= iota((L, L), 1)
     tril = ones_where(causal)
@@ -93,7 +104,7 @@
     tile = ones_where(iota((state, per * state), 0) == iota((state, per * state), 1) % state)
     quad = 4 * head
 
-    for copy in loads:
+    for copy in loads[:3]:
         copy.wait()
     cum, cum_t, e_exp, t_exp, ce, be, b_t, c_t = [], [], [], [], [], [], [], []
     for c in range(chunks):
@@ -107,26 +118,9 @@
         b_t.append(bt)
         c_t.append(ct)
         pex[c] = jnp.exp(exact_right(cu[L - 8:, :], by_col))
-        et = jnp.exp(cut)
-        tt = jnp.exp(cut[:, L - 1:] - cut)
-        for k in range(width // quad):
-            lanes = pl.ds(k * quad, quad)
-            lhs_b = jnp.concatenate([bt * tt[h:h + 1, :] for h in range(4 * k, 4 * k + 4)], 0).astype(BF16)
-            lhs_c = jnp.concatenate([ct * et[h:h + 1, :] for h in range(4 * k, 4 * k + 4)], 0).astype(BF16)
-            rb = dot(lhs_b, x_ref[at, lanes])
-            rc = dot(lhs_c, g_ref[at, lanes])
-            which = iota((state, quad), 1) // head
-            ob = rb[:state]
-            oc = rc[:state]
-            for h in range(1, 4):
-                ob = jnp.where(which == h, rb[h * state:(h + 1) * state], ob)
-                oc = jnp.where(which == h, rc[h * state:(h + 1) * state], oc)
-            own[c, k * quad // wide, :, (k * quad) % wide:(k * quad) % wide + quad] = ob
-            gown[c, k * quad // wide, :, (k * quad) % wide:(k * quad) % wide + quad] = oc
-
-    pl.semaphore_wait(
-        barrier, peers - 1 + jnp.minimum(place, 1) + jnp.minimum(hops - 1 - place, 1)
-    )
+    pl.semaphore_wait(barrier, peers - 1 + near)
+    for copy in loads[3:]:
+        copy.wait()
 
     def decay(c, k):
         return pex[c, 7:8, k * wide:(k + 1) * wide]
@@ -143,56 +137,147 @@
             device_id={"dp": place - 1}, device_id_type=MESH,
         )
 
-    def relay(first):
-        for k in range(PIECES):
-            @pl.when(place == 0 if first else place > 0)
-            def _():
-                if first:
-                    fin[k] = jnp.zeros(fin.shape[1:], F32)
-                else:
-                    f_copy(k).wait_recv()
-
-            @pl.when(place < hops - 1)
-            def _():
-                s = own[0, k] if first else decay(0, k) * fin[k] + own[0, k]
-                for c in range(1, chunks):
-                    s = decay(c, k) * s + own[c, k]
-                fout[k] = s
-                f_copy(k).start()
-
-    def relay_back(first):
-        for k in range(PIECES):
-            @pl.when(place == hops - 1 if first else place < hops - 1)
-            def _():
-                if first:
-                    gin[k] = jnp.zeros(gin.shape[1:], F32)
-                else:
-                    b_copy(k).wait_recv()
-
-            @pl.when(place > 0)
-            def _():
-                last = chunks - 1
-                s = gown[last, k] if first else decay(last, k) * gin[k] + gown[last, k]
-                for c in range(chunks - 2, -1, -1):
-                    s = decay(c, k) * s + gown[c, k]
-                gout[k] = s
-                b_copy(k).start()
-
-    stages = min(hops, 4)
+    def send(k):
+        s = decay(0, k) * fin[k] + own[0, k]
+        for c in range(1, chunks):
+            s = decay(c, k) * s + own[c, k]
+        fout[k] = s
+        f_copy(k).start()
+
+    def send_back(k):
+        s = decay(chunks - 1, k) * gin[k] + gown[chunks - 1, k]
+        for c in range(chunks - 2, -1, -1):
+            s = decay(c, k) * s + gown[c, k]
+        gout[k] = s
+        b_copy(k).start()
+
+    stages = max(min(hops, 4), 2)
     from_end = hops - 1 - place
 
-    def exchange(stage):
-        when = (lambda v: v >= stage) if stage == stages - 1 else (lambda v: v == stage)
-
-        @pl.when(when(place))
+    def forth(stage, k):
+        last = stage == stages - 1
+
+        @pl.when(place >= stage if last else place == stage)
         def _():
-            relay(stage == 0)
-
-        @pl.when(when(from_end))
+            if stage:
+                f_copy(k).wait_recv()
+            else:
+                fin[k] = jnp.zeros(fin.shape[1:], F32)
+            pl.when(place < hops - 1)(lambda: send(k))
+
+    def back(stage, k):
+        last = stage == stages - 1
+
+        @pl.when(from_end >= stage if last else from_end == stage)
         def _():
-            relay_back(stage == 0)
-
-    exchange(0)
+            if stage:
+                b_copy(k).wait_recv()
+            else:
+                gin[k] = jnp.zeros(gin.shape[1:], F32)
+            pl.when(place > 0)(lambda: send_back(k))
+
+    def two_step(forward):
+        if forward:
+            at, out, into, mine_own, order = place, fout, fin, own, range(chunks)
+            far, far_in, sems = ffar, ffar_in, (fsend, frecv, fsend2, frecv2)
+        else:
+            at, out, into, mine_own, order = from_end, gout, gin, gown, range(chunks - 1, -1, -1)
+            far, far_in, sems = bfar, bfar_in, (bsend, brecv, bsend2, brecv2)
+        send_sem, recv_sem, send2_sem, recv2_sem = sems
+
+        def link(src, dst, sent, got, to, k):
+            return pltpu.make_async_remote_copy(
+                src_ref=src.at[k], dst_ref=dst.at[k], send_sem=sent.at[k], recv_sem=got.at[k],
+                device_id={"dp": to if forward else hops - 1 - to}, device_id_type=MESH,
+            )
+
+        def total(k, before=None):
+            value = before
+            for c in order:
+                value = mine_own[c, k] if value is None else decay(c, k) * value + mine_own[c, k]
+            return value
+
+        def step(stage, k):
+            if stage == 0:
+                @pl.when(at == 0)
+                def _():
+                    into[k] = jnp.zeros(into.shape[1:], F32)
+                    out[k] = total(k)
+                    link(out, into, send_sem, recv_sem, 1, k).start()
+
+                @pl.when(at == 2)
+                def _():
+                    through = decay(0, k)
+                    for c in range(1, chunks):
+                        through = through * decay(c, k)
+                    far[k, :state] = total(k)
+                    far[k, state:] = jnp.broadcast_to(through, (8, wide))
+                    link(far, far_in, send2_sem, recv2_sem, 3, k).start()
+
+            if stage == 1:
+                @pl.when(at == 1)
+                def _():
+                    link(out, into, send_sem, recv_sem, 2, k).wait_recv()
+                    out[k] = total(k, into[k])
+                    link(out, into, send2_sem, recv_sem, 3, k).start()
+                    link(out, into, send_sem, recv_sem, 2, k).start()
+
+            if stage == 2:
+                @pl.when(at >= 2)
+                def _():
+                    link(out, into, send_sem, recv_sem, 1, k).wait_recv()
+
+                @pl.when(at == 3)
+                def _():
+                    link(far, far_in, send2_sem, recv2_sem, 3, k).wait_recv()
+                    into[k] = far_in[k, state:state + 1] * into[k] + far_in[k, :state]
+
+        def sent():
+            for k in range(PIECES):
+                @pl.when(at <= 1)
+                def _():
+                    link(out, into, send_sem, recv_sem, 2, k).wait_send()
+
+                @pl.when(at == 1)
+                def _():
+                    link(out, into, send2_sem, recv_sem, 3, k).wait_send()
+
+                @pl.when(at == 2)
+                def _():
+                    link(far, far_in, send2_sem, recv2_sem, 3, k).wait_send()
+
+        return step, sent
+
+    if short:
+        stages = 3
+        forth, forth_sent = two_step(True)
+        back, back_sent = two_step(False)
+
+    which = iota((state, quad), 1) // head
+    e_t = [jnp.exp(cut) for cut in cum_t]
+    s_t = [jnp.exp(cut[:, L - 1:] - cut) for cut in cum_t]
+
+    def own_part(scaled, by, values, heads_of):
+        lhs = jnp.concatenate([scaled * by[h:h + 1, :] for h in heads_of], 0).astype(BF16)
+        r = dot(lhs, values)
+        out = r[:state]
+        for h in range(1, 4):
+            out = jnp.where(which == h, r[h * state:(h + 1) * state], out)
+        return out
+
+    def own_piece(k, into, scaled, by, values):
+        for c in range(chunks):
+            for j in range(0, wide, quad):
+                first = (k * wide + j) // head
+                part = values[c * L:(c + 1) * L, k * wide + j:k * wide + j + quad]
+                into[c, k, :, j:j + quad] = own_part(scaled[c], by[c], part, range(first, first + 4))
+
+    for k in range(PIECES):
+        own_piece(k, gown, c_t, e_t, g_ref)
+        back(0, k)
+    for k in range(PIECES):
+        own_piece(k, own, b_t, s_t, x_ref)
+        forth(0, k)
 
     scores, grad_scores = [], []
     for c in range(chunks):
@@ -215,10 +300,16 @@
     left = ones_where(iota((L, pair), 1) < head)
     right = ones_where(iota((L, pair), 1) >= head)
     units = [(c, p) for p in range(width // pair) for c in range(chunks)]
+    def between(n):
+        for stage in range(1, stages - 1):
+            if n == (4 if stage == 1 else 24):
+                for k in range(PIECES):
+                    back(stage, k)
+                for k in range(PIECES):
+                    forth(stage, k)
+
     for n, (c, p) in enumerate(units):
-        for stage in range(1, stages):
-            if n == len(units) * stage // (stages - 1) - 1 and stage < stages - 1:
-                exchange(stage)
+        between(n)
         at = pl.ds(c * L, L)
         lanes = pl.ds(p * pair, pair)
         weights = []
@@ -234,14 +325,29 @@
         dxs[at, lanes] = dot(jnp.concatenate(mix, 0), g2, TN)
         dm = dot(g, x2, NT)
         grad_scores[c] += weights[0] * dm[:, :L] + weights[1] * dm[:, L:]
-    if stages > 1:
-        exchange(stages - 1)
+    between(len(units))
 
     block = ones_where(iota((per * state, wide), 0) // state == iota((per * state, wide), 1) // head)
     acc_c = [jnp.zeros((L, per * state), F32) for _ in range(chunks)]
     acc_b = [jnp.zeros((L, per * state), F32) for _ in range(chunks)]
+    dcum = [jnp.zeros((heads, L), F32) for _ in range(chunks)]
     ends = []
+
+    def finish(k):
+        for c in range(chunks):
+            at = pl.ds(c * L, L)
+            cols = pl.ds(k * wide, wide)
+            y = ys[at, cols] + dot(ce[c][k], sbd[c, k])
+            dx = dxs[at, cols] + dot(be[c][k], gbd[c, k])
+            yz_ref[0, at, cols] = y.astype(BF16)
+            yz_ref[1, at, cols] = dx.astype(BF16)
+            q = g_ref[at, cols].astype(F32) * y - x_ref[at, cols].astype(F32) * dx
+            q += jnp.where(iota((L, wide), 0) == L - 1, ends[k][c], 0.0)
+            dcum[c] += exact_left(by_col[:, k * wide:(k + 1) * wide], q, NT, 2)
+
     for k in range(PIECES):
+        back(stages - 1, k)
+        forth(stages - 1, k)
         states = [fin[k]]
         for c in range(chunks):
             states.append(decay(c, k) * states[c] + own[c, k])
@@ -260,6 +366,8 @@
             gbd[c, k] = r2
             acc_c[c] += dot(g_ref[at, cols], s2, NT) * e_exp[c][:, lanes]
             acc_b[c] += dot(x_ref[at, cols], r2, NT) * t_exp[c][:, lanes]
+        if k:
+            finish(k - 1)
 
     for c in range(chunks):
         ds = jnp.where(causal, grad_scores[c], 0.0)
@@ -275,19 +383,9 @@
     for d in range(1, peers):
         m_copy(d, mine).start()
 
+    finish(PIECES - 1)
     for c in range(chunks):
-        at = pl.ds(c * L, L)
-        dcum = jnp.zeros((heads, L), F32)
-        for k in range(PIECES):
-            cols = pl.ds(k * wide, wide)
-            y = ys[at, cols] + dot(ce[c][k], sbd[c, k])
-            dx = dxs[at, cols] + dot(be[c][k], gbd[c, k])
-            yz_ref[0, at, cols] = y.astype(BF16)
-            yz_ref[1, at, cols] = dx.astype(BF16)
-            q = g_ref[at, cols].astype(F32) * y - x_ref[at, cols].astype(F32) * dx
-            q += jnp.where(iota((L, wide), 0) == L - 1, ends[k][c], 0.0)
-            dcum += exact_left(by_col[:, k * wide:(k + 1) * wide], q, NT, 2)
-        small_ref[2 * state:, at] = exact_right(dcum, tril)
+        small_ref[2 * state:, c * L:(c + 1) * L] = exact_right(dcum[c], tril)
 
     for d in range(1, peers):
         m_copy(d, lax.rem(mine + peers - d, peers)).wait_recv()
@@ -296,6 +394,11 @@
     for d in range(1, peers):
         total += mall[d]
     small_ref[:2 * state] = total
+
+    if short:
+        forth_sent()
+        back_sent()
+        return
 
     @pl.when(place < hops - 1)
     def _():
@@ -349,6 +452,14 @@
             pltpu.SemaphoreType.DMA((PIECES,)),
             pltpu.SemaphoreType.DMA((peers - 1,)),
             pltpu.SemaphoreType.DMA((peers - 1,)),
+            pltpu.VMEM((PIECES, state + 8, wide), F32),
+            pltpu.VMEM((PIECES, state + 8, wide), F32),
+            pltpu.VMEM((PIECES, state + 8, wide), F32),
+            pltpu.VMEM((PIECES, state + 8, wide), F32),
+            pltpu.SemaphoreType.DMA((PIECES,)),
+            pltpu.SemaphoreType.DMA((PIECES,)),
+            pltpu.SemaphoreType.DMA((PIECES,)),
+            pltpu.SemaphoreType.DMA((PIECES,)),
         ],
         compiler_params=pltpu.CompilerParams(
             collective_id=0, has_side_effects=True, vmem_limit_bytes=40 * 2**20

time: 24.5 us -> 23 us (0.939)
  Pallas kernels: 20.9 us -> 19.4 us
    pallas_call x1, Pallas kernels: 20.9 us -> 19.4 us  [local(): pl.pallas_call(functools.partial(kernel, hops, peers, heads), out_shape=(...]
where the time goes in v3:
time: 23 us; the launch traced here: 22.8 us
  Pallas kernels  19.4 us (84%)
  local copies, waits for them, and re-layouts  2.8 us (12%)
  between operations  0.64 us (3%)
    pallas_call x1, Pallas kernels, local(): pl.pallas_call(functools.partial(kernel, hops, peers, heads), out_shape=(...  19.4 us
    squeeze x1, local copies, waits for them, and re-layouts, local(): yz[1]  1.57 us
    transpose x1, local copies, waits for them, and re-layouts, local(): small[2 * state:]  0.62 us
    transpose x1, local copies, waits for them, and re-layouts, local(): small[:state]  0.61 us

profile of v3, /device:TPU:0, one launch (start us, length us, event | category | flops | bytes accessed | tf_op | source)
XLA Modules:
  0.0 22.8 jit_solution(1071998603360424748)
XLA Ops:
  0.6 19.4 %shard_map.92 = (bf16[2,256,2048]{2,1,0:T(8,128)(2,1)S(1)}, f32[64,256]{1,0:T(8,128)S(1)}) custom-call(bf16[256,2048]{1,0:T(8,128)(2,1)} %x_hbm.1, f32[32,256]{1,0:T(8,128)} %bitcast.13, f32[16,256]{1,0:T(8,128)} %bitcast.14, f32[16,256]{1,0:T(8,128)} %bitcast.15, bf16[256,2048]{1,0:T(8,128)(2,1)} %g_hbm.1), custom_call_target="tpu_custom_call" | custom-call | tf_op jit(solution)/shard_map/pallas_call | solution.py:422
  20.0 1.6 %slice_bitcast_fusion = (bf16[256,2048]{1,0:T(8,128)(2,1)}, bf16[256,2048]{1,0:T(8,128)(2,1)}) fusion(bf16[2,256,2048]{2,1,0:T(8,128)(2,1)S(1)} %get-tuple-element.7), kind=kLoop, calls=%fused_computation | loop fusion | bytes 4194304 | tf_op jit(solution)/shard_map/squeeze | solution.py:468
  21.6 0.6 %slice_bitcast_fusion.2 = f32[256,32]{0,1:T(8,128)} fusion(f32[64,256]{1,0:T(8,128)S(1)} %get-tuple-element.8), kind=kLoop, calls=%fused_computation.2 | loop fusion | bytes 65536 | tf_op jit(solution)/shard_map/transpose | solution.py:468
  22.2 0.6 %slice_bitcast_fusion.3 = (f32[256,16]{0,1:T(8,128)}, f32[256,16]{0,1:T(8,128)}) fusion(f32[64,256]{1,0:T(8,128)S(1)} %get-tuple-element.8), kind=kLoop, calls=%fused_computation.3 | loop fusion | bytes 65536 | tf_op jit(solution)/shard_map/transpose | solution.py:468

commit v4 on v3

--- a/solution.py
+++ b/solution.py
@@ -64,7 +64,7 @@
     loads = [
         pltpu.make_async_copy(src, dst, load.at[i])
         for i, (src, dst) in enumerate(
-            [(ld_hbm, ld_ref), (b_hbm, b_ref), (c_hbm, c_ref), (x_hbm, x_ref), (g_hbm, g_ref)]
+            [(ld_hbm, ld_ref), (b_hbm, b_ref), (c_hbm, c_ref), (g_hbm, g_ref), (x_hbm, x_ref)]
         )
     ]
     for copy in loads:
@@ -119,8 +119,7 @@
         c_t.append(ct)
         pex[c] = jnp.exp(exact_right(cu[L - 8:, :], by_col))
     pl.semaphore_wait(barrier, peers - 1 + near)
-    for copy in loads[3:]:
-        copy.wait()
+    loads[3].wait()
 
     def decay(c, k):
         return pex[c, 7:8, k * wide:(k + 1) * wide]
@@ -275,6 +274,7 @@
     for k in range(PIECES):
         own_piece(k, gown, c_t, e_t, g_ref)
         back(0, k)
+    loads[4].wait()
     for k in range(PIECES):
         own_piece(k, own, b_t, s_t, x_ref)
         forth(0, k)
@@ -302,7 +302,7 @@
     units = [(c, p) for p in range(width // pair) for c in range(chunks)]
     def between(n):
         for stage in range(1, stages - 1):
-            if n == (4 if stage == 1 else 24):
+            if n == (0 if stage == 1 else 24):
                 for k in range(PIECES):
                     back(stage, k)
                 for k in range(PIECES):

time: 23 us -> 23.2 us (level)
  the two profiles are of different devices: /device:TPU:0 before, /device:TPU:9 now
where the time goes in v4:
time: 23.2 us; the launch traced here: 23.1 us
  Pallas kernels  19.6 us (84%)
  local copies, waits for them, and re-layouts  2.8 us (12%)
  between operations  0.64 us (3%)
    pallas_call x1, Pallas kernels, local(): pl.pallas_call(functools.partial(kernel, hops, peers, heads), out_shape=(...  19.6 us
    squeeze x1, local copies, waits for them, and re-layouts, local(): yz[1]  1.57 us
    transpose x1, local copies, waits for them, and re-layouts, local(): small[2 * state:]  0.62 us
    transpose x1, local copies, waits for them, and re-layouts, local(): small[:state]  0.61 us

profile of v4, /device:TPU:9, one launch (start us, length us, event | category | flops | bytes accessed | tf_op | source)
XLA Modules:
  0.0 23.1 jit_solution(12653824107738004593)
XLA Ops:
  0.6 19.6 %shard_map.92 = (bf16[2,256,2048]{2,1,0:T(8,128)(2,1)S(1)}, f32[64,256]{1,0:T(8,128)S(1)}) custom-call(bf16[256,2048]{1,0:T(8,128)(2,1)} %x_hbm.1, f32[32,256]{1,0:T(8,128)} %bitcast.13, f32[16,256]{1,0:T(8,128)} %bitcast.14, f32[16,256]{1,0:T(8,128)} %bitcast.15, bf16[256,2048]{1,0:T(8,128)(2,1)} %g_hbm.1), custom_call_target="tpu_custom_call" | custom-call | tf_op jit(solution)/shard_map/pallas_call | solution.py:422
  20.3 1.6 %slice_bitcast_fusion = (bf16[256,2048]{1,0:T(8,128)(2,1)}, bf16[256,2048]{1,0:T(8,128)(2,1)}) fusion(bf16[2,256,2048]{2,1,0:T(8,128)(2,1)S(1)} %get-tuple-element.7), kind=kLoop, calls=%fused_computation | loop fusion | bytes 4194304 | tf_op jit(solution)/shard_map/squeeze | solution.py:468
  21.8 0.6 %slice_bitcast_fusion.2 = f32[256,32]{0,1:T(8,128)} fusion(f32[64,256]{1,0:T(8,128)S(1)} %get-tuple-element.8), kind=kLoop, calls=%fused_computation.2 | loop fusion | bytes 65536 | tf_op jit(solution)/shard_map/transpose | solution.py:468
  22.5 0.6 %slice_bitcast_fusion.3 = (f32[256,16]{0,1:T(8,128)}, f32[256,16]{0,1:T(8,128)}) fusion(f32[64,256]{1,0:T(8,128)S(1)} %get-tuple-element.8), kind=kLoop, calls=%fused_computation.3 | loop fusion | bytes 65536 | tf_op jit(solution)/shard_map/transpose | solution.py:468
